TPU v7x, 512 devices: a whole 4x4x16 slice. The times are simulated.
512 devices in a mesh: row: 32 (over x_lo, z), col: 16 (over y, x_hi, core).
Axes of the slice: x: 4 (x_hi: 2, x_lo: 2; x = x_hi * 2 + x_lo), y: 4, z: 16, core: 2. Of those that a mesh axis runs over, the one named last changes fastest.
Arguments:
- row_features: bfloat16 [98304, 256], P('row'), may hold values from -6 to 6
- row_vectors: bfloat16 [17, 98304], P(None, 'row'), may hold values from -24 to 24
- slab_features: bfloat16 [3072, 256], P('col', 'row'), may hold values from -6 to 6
- slab_vectors: bfloat16 [17, 3072], P(None, 'col'), may hold values from -24 to 24
Outputs:
- row_grad: float32 [98304, 256], P('row', 'col')
- slab_grad: float32 [3072, 256], P('col', 'row')
All inputs are finite; a program needn't handle non-finite values.
Results may differ from a plain program's by a relative error of at most 0.008.
Values may be sent and summed in bfloat16 or wider, within the bound.
A program may use at most 64 MiB of HBM per device.

v0:
```python
import jax
import jax.numpy as jnp
from jax import lax
from jax.sharding import PartitionSpec as P

D = 256
PROBES = 16
VECS = 17


def weighted(features, vectors, block, block_vectors):
    left_square = jnp.sum(jnp.square(features.astype(jnp.float32)), axis=1)
    right_square = jnp.sum(jnp.square(block.astype(jnp.float32)), axis=1)
    inner = lax.dot_general(
        features, block, (((1,), (1,)), ((), ())), preferred_element_type=jnp.float32
    )
    distance = left_square[:, None] + right_square[None, :] - 2.0 * inner
    kernel = jnp.exp(-distance / (2.0 * D))
    factors = jnp.where(jnp.arange(VECS) == 0, 0.5, -0.5 / PROBES)
    scaled = (block_vectors.astype(jnp.float32) * factors[:, None]).astype(jnp.bfloat16)
    coupling = jnp.einsum("kr,kc->rc", vectors, scaled, preferred_element_type=jnp.float32)
    return (coupling * kernel).astype(jnp.bfloat16)


def slab_side(weights, features, block):
    wide_cols = jnp.sum(weights.astype(jnp.float32), axis=0)
    product = lax.dot_general(
        weights, features, (((0,), (0,)), ((), ())), preferred_element_type=jnp.float32
    )
    return (product - wide_cols[:, None] * block.astype(jnp.float32)) / D


def local(row_features, row_vectors, slab_features, slab_vectors):
    columns = lax.all_gather(slab_features, "row", axis=1, tiled=True)
    weights = weighted(row_features, row_vectors, columns, slab_vectors)
    wide_rows = jnp.sum(weights.astype(jnp.float32), axis=1)
    product = jnp.dot(weights, columns, preferred_element_type=jnp.float32)
    row_term = (product - wide_rows[:, None] * row_features.astype(jnp.float32)) / D
    row_grad = lax.psum_scatter(row_term, "col", scatter_dimension=1, tiled=True)
    partial_slab = slab_side(weights, row_features, columns)
    slab_grad = lax.psum_scatter(partial_slab, "row", scatter_dimension=1, tiled=True)
    return (row_grad, slab_grad)


def solution(mesh):
    return jax.shard_map(
        local,
        mesh=mesh,
        in_specs=(P("row", None), P(None, "row"), P("col", "row"), P(None, "col")),
        out_specs=(P("row", "col"), P("col", "row")),
        check_vma=False,
    )
```

profile of v0, /device:TPU:8, one launch (start us, length us, event | category | flops | bytes accessed | tf_op | source)
XLA Modules:
  0.0 311.2 jit_solution(13705534259267237124)
XLA Ops:
  7.2 0.0 copy-start
  7.2 0.0 reduce-scatter.5.cloned.1.call-start
  7.2 69.7 %all_gather.3 = bf16[192,256]{0,1:T(8,128)(2,1)S(1)} all-gather(bf16[192,8]{0,1:T(8,128)(2,1)} %param.6), channel_id=1, replica_groups=mesh['row'=32,'col'=16] {'row'}, dimensions={1}, use_global_device_ids=true | all-gather | bytes 101376 | tf_op jit(solution)/shard_map/all_gather | solution.py:34
  76.9 0.1 fusion.9
  77.0 0.0 copy-start.1
  77.0 1.8 copy.6
  78.8 0.3 fusion.7
  79.2 0.0 copy-done.1
  79.2 0.0 copy-start.3
  79.2 0.8 fusion.5
  80.0 0.0 copy-done
  80.0 0.0 copy-done.3
  80.0 0.0 copy-start.2
  80.0 0.7 convert_reduce_fusion
  80.7 0.7 copy-done.2
  81.4 1.5 fusion.8
  82.9 0.0 reduce-scatter.5.cloned.1.call-update
  82.9 0.0 reduce-scatter.3.cloned.1.call-start
  82.9 2.3 fusion
  85.2 0.0 reduce-scatter.3.cloned.1.call-update
  85.2 123.7 %reduce-scatter.5.cloned.1.call-done = f32[192,8]{0,1:T(8,128)} async-done(((f32[192,256]{0,1:T(8,128)}), f32[192,8]{0,1:T(8,128)}) %reduce-scatter.5.cloned.1.call-update) | async-done | bytes 6160 | tf_op jit(solution)/shard_map/reduce_scatter | solution.py:41
  208.9 95.4 %reduce-scatter.3.cloned.1.call-done = f32[3072,16]{0,1:T(8,128)} async-done(((f32[3072,256]{0,1:T(8,128)}), f32[3072,16]{0,1:T(8,128)}) %reduce-scatter.3.cloned.1.call-update) | async-done | bytes 196624 | tf_op jit(solution)/shard_map/reduce_scatter | solution.py:39
  (1 shorter events, 0.0 us)
Async XLA Ops:
  7.2 72.8 %copy-start = (bf16[17,3072]{1,0:T(8,128)(2,1)S(1)}, bf16[17,3072]{1,0:T(8,128)(2,1)}, u32[]{:S(2)}) copy-start(bf16[17,3072]{1,0:T(8,128)(2,1)} %param.5) | copy-start | bytes 313348
  7.2 201.7 %reduce-scatter.5.cloned.1.call-start = ((), (), s32[]{:S(2)}) async-start(), calls=%async_computation.3 | async-start | bytes 270336 | tf_op jit(solution)/shard_map/reduce_scatter | solution.py:41
  77.0 2.2 copy-start.1
  79.2 0.8 copy-start.3
  80.0 1.4 copy-start.2
  82.9 221.5 %reduce-scatter.3.cloned.1.call-start = ((), (), s32[]{:S(2)}) async-start(), calls=%async_computation.2 | async-start | bytes 3342336 | tf_op jit(solution)/shard_map/reduce_scatter | solution.py:39
Sparse Core Ops, SparseCore 0:
  83.0 125.8 reduce-scatter.4
  215.2 89.1 reduce-scatter.2
where the time goes:
time: 311 us
  waiting for transfers between devices  219 us (70%)
  blocking collectives  69.7 us (22%)
  between operations  14.1 us (5%)
  matrix products  5.17 us (2%)
    reduce_scatter x1, waiting for transfers between devices, local(): lax.psum_scatter(partial_slab, 'row', scatter_dimension=1, tiled=True)  124 us
    reduce_scatter x1, waiting for transfers between devices, local(): lax.psum_scatter(row_term, 'col', scatter_dimension=1, tiled=True)  95.4 us
    all_gather x1, blocking collectives, local(): columns = lax.all_gather(slab_features, 'row', axis=1, tiled=True)  69.7 us
  transfers between devices with their start and end apart: 2, of which 2 were waited for; matrix products, arithmetic and copies ran while one was open for 1% of the time, Pallas kernels for 0%

commit v1 on v0

v1 whole, which is shorter than its diff:
```python
import functools

import jax
import jax.numpy as jnp
from jax import lax
from jax.experimental import pallas as pl
from jax.experimental.pallas import tpu as pltpu
from jax.sharding import PartitionSpec as P

D = 256
PROBES = 16
VECS = 17
ROWS = 3072
COLS = 192
N_ROW = 32
CHUNKS = 6
RQ = ROWS // CHUNKS
LAG = (2, 4, 6, 8)
F32, BF16 = jnp.float32, jnp.bfloat16


def kernel(
    sf, sv, rv, rf_hbm,
    row_out, slab_out,
    rf, rft, rsq, coup, slots, slabn, slabp, ssq, acc, wcol,
    kept, s_a, r_a, s_bp, r_bp, s_bm, r_bm, s_cp, r_cp, s_cm, r_cm, s_d, r_d,
    g_own, g_send, g_recv,
    rf_sem, ag_send, ag_recv, g_ssem, g_rsem, st_send, st_recv,
):
    row, col = lax.axis_index("row"), lax.axis_index("col")
    y, hi, core = col // 4, lax.rem(col // 2, 2), lax.rem(col, 2)
    up, down, far = lax.rem(y + 1, 4), lax.rem(y + 3, 4), lax.rem(y + 2, 4)

    def at(y_, hi_, core_):
        return {"row": row, "col": y_ * 4 + hi_ * 2 + core_}

    sibling = at(y, hi, 1 - core)
    above, below, across = at(up, hi, core), at(down, hi, core), at(y, 1 - hi, core)

    load = pltpu.make_async_copy(rf_hbm, rf, rf_sem)
    load.start()

    barrier = pltpu.get_barrier_semaphore()
    for other in (sibling, above, below, across):
        pl.semaphore_signal(barrier, inc=1, device_id=other)

    def greet(d, c):
        pl.semaphore_signal(
            barrier, inc=1, device_id={"row": lax.rem(row + d, N_ROW), "col": col}
        )
        return c

    lax.fori_loop(1, N_ROW, greet, 0)
    pl.semaphore_wait(barrier, N_ROW + 3)

    def gather(peer, slot):
        return pltpu.make_async_remote_copy(
            sf, slots.at[slot], ag_send.at[peer], ag_recv.at[slot],
            device_id={"row": peer, "col": col},
        )

    def send_slab(d, c):
        gather(lax.rem(row + d, N_ROW), row).start()
        return c

    lax.fori_loop(1, N_ROW, send_slab, 0)
    slots[row] = sf[...]

    first = lax.broadcasted_iota(jnp.int32, (VECS, COLS), 0) == 0
    scaled = (sv[...].astype(F32) * jnp.where(first, 0.5, -0.5 / PROBES)).T.astype(BF16)
    load.wait()

    def prepare(q, c):
        wide = rf[pl.ds(pl.multiple_of(q * RQ, RQ), RQ), :].astype(F32).T
        rsq[q] = jnp.sum(wide * wide, axis=0, keepdims=True) * (0.5 / D)
        rft[q] = wide.astype(BF16)
        coup[q] = jnp.dot(
            scaled, rv[:, pl.ds(pl.multiple_of(q * RQ, RQ), RQ)],
            preferred_element_type=F32,
        )
        return c

    lax.fori_loop(0, CHUNKS, prepare, 0)
    acc[...] = jnp.zeros_like(acc)
    wcol[...] = jnp.zeros_like(wcol)

    def got_slab(d, c):
        peer = lax.rem(row + d, N_ROW)
        gather(peer, peer).wait_recv()
        return c

    lax.fori_loop(1, N_ROW, got_slab, 0)

    slab_t = slots[...].astype(F32).reshape(D, COLS)
    slab_n = slab_t.T
    ssq[...] = jnp.broadcast_to(
        jnp.sum(slab_n * slab_n, axis=1, keepdims=True) * (0.5 / D), ssq.shape
    )
    slabn[...] = (slab_n * (1.0 / D)).astype(BF16)
    order = [yy * 4 + hh * 2 + cc for cc in range(2) for yy in range(4) for hh in range(2)]
    slabp[...] = jnp.concatenate(
        [slab_t[g * 16 : g * 16 + 16] * (1.0 / D) for g in order], axis=0
    ).astype(BF16)

    def hop(stage, q, src, dst, to):
        return pltpu.make_async_remote_copy(
            src, dst, st_send.at[stage, q], st_recv.at[stage, q], device_id=to
        )

    def hop_a(q):
        return hop(0, q, s_a.at[q], r_a.at[q], sibling)

    def hop_bp(q):
        return hop(1, q, s_bp.at[q], r_bp.at[q], above)

    def hop_bm(q):
        return hop(2, q, s_bm.at[q], r_bm.at[q], below)

    def hop_cp(q):
        return hop(3, q, s_cp.at[q], r_cp.at[q], above)

    def hop_cm(q):
        return hop(4, q, s_cm.at[q], r_cm.at[q], below)

    def hop_d(q):
        return hop(5, q, s_d.at[q], r_d.at[q], across)

    def compute(q):
        feats = rft[q]
        inner = jnp.dot(slabn[...], feats, preferred_element_type=F32)
        gauss = jnp.exp(inner - rsq[q] - ssq[:, :1])
        w = (coup[q] * gauss).astype(BF16)
        wf = w.astype(F32)
        wide = jnp.sum(wf, axis=0, keepdims=True) * (1.0 / D)
        prod = jnp.dot(slabp[...], w, preferred_element_type=F32)
        halves = []
        for cc in range(2):
            own = jnp.concatenate(
                [
                    feats[g * 16 : g * 16 + 16].astype(F32)
                    for g in order[cc * 8 : cc * 8 + 8]
                ],
                axis=0,
            )
            halves.append(prod[cc * 128 : cc * 128 + 128] - wide * own)
        mine = core == 0
        kept[q] = jnp.where(mine, halves[0], halves[1]).reshape(4, 2, 16, RQ)
        s_a[q] = jnp.where(mine, halves[1], halves[0]).astype(BF16).reshape(4, 2, 16, RQ)
        hop_a(q).start()
        acc[...] += jnp.dot(
            w, rf[pl.ds(pl.multiple_of(q * RQ, RQ), RQ), :], preferred_element_type=F32
        )
        part = wf[:, :128]
        for lane in range(128, RQ, 128):
            part = part + wf[:, lane : lane + 128]
        wcol[...] += part

    def exchange(peer, slot):
        return pltpu.make_async_remote_copy(
            g_send.at[peer], g_recv.at[slot], g_ssem.at[peer], g_rsem.at[slot],
            device_id={"row": peer, "col": col},
        )

    def slab_side():
        total = jnp.sum(wcol[...], axis=1, keepdims=True)
        grad = acc[...] * (1.0 / D) - total * slabn[...].astype(F32)
        pieces = grad.T.reshape(N_ROW, 8, COLS)
        g_own[...] = pieces
        g_send[...] = pieces.astype(BF16)

        def send(d, c):
            exchange(lax.rem(row + d, N_ROW), row).start()
            return c

        lax.fori_loop(1, N_ROW, send, 0)
        g_recv[row] = jnp.zeros((8, COLS), BF16)

    def stage_b(q):
        hop_a(q).wait_recv()
        total = kept[q] + r_a[q].astype(F32)
        kept[q] = total
        s_bp[q] = kept[q, far, 0].astype(BF16)
        s_bm[q] = kept[q, far, 1].astype(BF16)
        hop_bp(q).start()
        hop_bm(q).start()

    def stage_c(q):
        hop_bp(q).wait_recv()
        s_cp[q, 0] = (kept[q, up, 0] + r_bp[q].astype(F32)).astype(BF16)
        s_cp[q, 1] = kept[q, up, 1].astype(BF16)
        hop_cp(q).start()
        hop_bm(q).wait_recv()
        s_cm[q, 0] = kept[q, down, 0].astype(BF16)
        s_cm[q, 1] = (kept[q, down, 1] + r_bm[q].astype(F32)).astype(BF16)
        hop_cm(q).start()

    def stage_d(q):
        hop_cp(q).wait_recv()
        hop_cm(q).wait_recv()
        there, here = 1 - hi, hi
        s_d[q] = (
            kept[q, y, there] + r_cp[q, there].astype(F32) + r_cm[q, there].astype(F32)
        ).astype(BF16)
        hop_d(q).start()
        kept[q, y, here] = (
            kept[q, y, here] + r_cp[q, here].astype(F32) + r_cm[q, here].astype(F32)
        )

    def stage_e(q):
        hop_d(q).wait_recv()
        row_out[:, pl.ds(pl.multiple_of(q * RQ, RQ), RQ)] = kept[q, y, hi] + r_d[
            q
        ].astype(F32)

    def step(t, c):
        pl.when(t < CHUNKS)(lambda: compute(t))
        pl.when(t == CHUNKS - 1)(slab_side)
        for lag, stage in zip(LAG, (stage_b, stage_c, stage_d, stage_e)):
            q = t - lag

            @pl.when((q >= 0) & (q < CHUNKS))
            def _(q=q, stage=stage):
                stage(q)

        return c

    lax.fori_loop(0, CHUNKS + LAG[-1], step, 0)

    def got_grad(d, c):
        peer = lax.rem(row + d, N_ROW)
        exchange(peer, peer).wait_recv()
        return c

    lax.fori_loop(1, N_ROW, got_grad, 0)
    slab_out[...] = g_own[row] + jnp.sum(g_recv[...].astype(F32), axis=0)

    def sent(d, c):
        peer = lax.rem(row + d, N_ROW)
        gather(peer, row).wait_send()
        exchange(peer, row).wait_send()
        return c

    lax.fori_loop(1, N_ROW, sent, 0)

    def sent_rows(q, c):
        for h in (hop_a, hop_bp, hop_bm, hop_cp, hop_cm, hop_d):
            h(q).wait_send()
        return c

    lax.fori_loop(0, CHUNKS, sent_rows, 0)


def local(row_features, row_vectors, slab_features, slab_vectors):
    vmem = pl.BlockSpec(memory_space=pltpu.VMEM)
    dma = pltpu.SemaphoreType.DMA
    small = lambda dtype: pltpu.VMEM((CHUNKS, 16, RQ), dtype)
    pair = lambda dtype: pltpu.VMEM((CHUNKS, 2, 16, RQ), dtype)
    half = lambda dtype: pltpu.VMEM((CHUNKS, 4, 2, 16, RQ), dtype)
    row_t, slab_t = pl.pallas_call(
        kernel,
        out_shape=(
            jax.ShapeDtypeStruct((16, ROWS), F32),
            jax.ShapeDtypeStruct((8, COLS), F32),
        ),
        in_specs=[vmem, vmem, vmem, pl.BlockSpec(memory_space=pl.ANY)],
        out_specs=(vmem, vmem),
        scratch_shapes=[
            pltpu.VMEM((ROWS, D), BF16),
            pltpu.VMEM((CHUNKS, D, RQ), BF16),
            pltpu.VMEM((CHUNKS, 1, RQ), F32),
            pltpu.VMEM((CHUNKS, COLS, RQ), F32),
            pltpu.VMEM((N_ROW, 8, COLS), BF16),
            pltpu.VMEM((COLS, D), BF16),
            pltpu.VMEM((D, COLS), BF16),
            pltpu.VMEM((COLS, 128), F32),
            pltpu.VMEM((COLS, D), F32),
            pltpu.VMEM((COLS, 128), F32),
            half(F32), half(BF16), half(BF16),
            small(BF16), small(BF16), small(BF16), small(BF16),
            pair(BF16), pair(BF16), pair(BF16), pair(BF16),
            small(BF16), small(BF16),
            pltpu.VMEM((N_ROW, 8, COLS), F32),
            pltpu.VMEM((N_ROW, 8, COLS), BF16),
            pltpu.VMEM((N_ROW, 8, COLS), BF16),
            dma, dma((N_ROW,)), dma((N_ROW,)), dma((N_ROW,)), dma((N_ROW,)),
            dma((6, CHUNKS)), dma((6, CHUNKS)),
        ],
        compiler_params=pltpu.CompilerParams(
            collective_id=0, has_side_effects=True, vmem_limit_bytes=40 * 1024 * 1024
        ),
        cost_estimate=pl.CostEstimate(
            flops=3 * 2 * ROWS * COLS * D, bytes_accessed=4_000_000,
            transcendentals=ROWS * COLS,
        ),
    )(slab_features.T, slab_vectors, row_vectors, row_features)
    return row_t.T, slab_t.T


def solution(mesh):
    return jax.shard_map(
        local,
        mesh=mesh,
        in_specs=(P("row", None), P(None, "row"), P("col", "row"), P(None, "col")),
        out_specs=(P("row", "col"), P("col", "row")),
        check_vma=False,
    )
```

time: 311 us -> 54.4 us (0.17)
  the two profiles are of different devices: /device:TPU:8 before, /device:TPU:4 now
where the time goes in v1:
time: 54.4 us; the launch traced here: 54.2 us
  Pallas kernels  48.5 us (89%)
  local copies, waits for them, and re-layouts  4.98 us (9%)
  between operations  0.65 us (1%)
    pallas_call x1, Pallas kernels, local(): pl.pallas_call(kernel, out_shape=(jax.ShapeDtypeStruct((16, ROWS), F32),...  48.5 us
    unnamed x10, local copies, waits for them, and re-layouts  4.98 us

profile of v1, /device:TPU:4, one launch (start us, length us, event | category | flops | bytes accessed | tf_op | source)
XLA Modules:
  0.0 54.2 jit_solution(7876504989981119626)
XLA Ops:
  0.6 0.0 copy-start
  0.6 1.4 %copy-done = bf16[3072,256]{1,0:T(8,128)(2,1)S(1)} copy-done((bf16[3072,256]{1,0:T(8,128)(2,1)S(1)}, bf16[3072,256]{1,0:T(8,128)(2,1)}, u32[]{:S(2)}) %copy-start) | copy-done | bytes 1572888
  2.0 0.0 copy-start.1
  2.0 0.9 %copy-done.1 = bf16[17,3072]{1,0:T(8,128)(2,1)S(1)} copy-done((bf16[17,3072]{1,0:T(8,128)(2,1)S(1)}, bf16[17,3072]{1,0:T(8,128)(2,1)}, u32[]{:S(2)}) %copy-start.1) | copy-done | bytes 104472
  3.0 0.0 copy-start.2
  3.0 0.7 %copy-done.2 = bf16[17,192]{1,0:T(8,128)(2,1)S(1)} copy-done((bf16[17,192]{1,0:T(8,128)(2,1)S(1)}, bf16[17,192]{1,0:T(8,128)(2,1)}, u32[]{:S(2)}) %copy-start.2) | copy-done | bytes 6552
  3.7 0.0 copy-start.3
  3.7 0.7 %copy-done.3 = bf16[192,8]{0,1:T(8,128)(2,1)S(1)} copy-done((bf16[192,8]{0,1:T(8,128)(2,1)S(1)}, bf16[192,8]{0,1:T(8,128)(2,1)}, u32[]{:S(2)}) %copy-start.3) | copy-done | bytes 3096
  4.3 48.5 %shard_map.59 = (f32[16,3072]{1,0:T(8,128)S(1)}, f32[8,192]{1,0:T(8,128)S(1)}) custom-call(bf16[8,192]{1,0:T(8,128)(2,1)S(1)} %bitcast.5, bf16[17,192]{1,0:T(8,128)(2,1)S(1)} %copy-done.2, bf16[17,3072]{1,0:T(8,128)(2,1)S(1)} %copy-done.1, bf16[3072,256]{1,0:T(8,128)(2,1)S(1)} %copy-done), custom_call_target="tpu_custom_call" | custom-call | flops 905969664 | bytes 4000000 | tf_op jit(solution)/shard_map/pallas_call | solution.py:259
  52.9 0.7 %copy.8 = f32[3072,16]{0,1:T(8,128)} copy(f32[3072,16]{0,1:T(8,128)S(1)} %bitcast.3) | data formatting | bytes 393216
  53.6 0.6 %copy.9 = f32[192,8]{0,1:T(8,128)} copy(f32[192,8]{0,1:T(8,128)S(1)} %bitcast.4) | data formatting | bytes 12288
Async XLA Ops:
  0.6 1.4 %copy-start = (bf16[3072,256]{1,0:T(8,128)(2,1)S(1)}, bf16[3072,256]{1,0:T(8,128)(2,1)}, u32[]{:S(2)}) copy-start(bf16[3072,256]{1,0:T(8,128)(2,1)} %rf_hbm.1) | copy-start | bytes 4718596
  2.0 0.9 %copy-start.1 = (bf16[17,3072]{1,0:T(8,128)(2,1)S(1)}, bf16[17,3072]{1,0:T(8,128)(2,1)}, u32[]{:S(2)}) copy-start(bf16[17,3072]{1,0:T(8,128)(2,1)} %rv.1) | copy-start | bytes 313348
  3.0 0.7 %copy-start.2 = (bf16[17,192]{1,0:T(8,128)(2,1)S(1)}, bf16[17,192]{1,0:T(8,128)(2,1)}, u32[]{:S(2)}) copy-start(bf16[17,192]{1,0:T(8,128)(2,1)} %sv.1) | copy-start | bytes 19588
  3.7 0.7 %copy-start.3 = (bf16[192,8]{0,1:T(8,128)(2,1)S(1)}, bf16[192,8]{0,1:T(8,128)(2,1)}, u32[]{:S(2)}) copy-start(bf16[192,8]{0,1:T(8,128)(2,1)} %param.6) | copy-start | bytes 9220

commit v2 on v0

v2 whole, which is shorter than its diff:
```python
import functools

import jax
import jax.numpy as jnp
from jax import lax
from jax.experimental import pallas as pl
from jax.experimental.pallas import tpu as pltpu
from jax.sharding import PartitionSpec as P

D = 256
PROBES = 16
VECS = 17
ROWS = 3072
COLS = 192
N_ROW = 32
CHUNKS = 3
RQ = ROWS // CHUNKS
LAG = 3
Z = 16
F32, BF16 = jnp.float32, jnp.bfloat16


def kernel(
    sf_hbm, sv_hbm, rv_hbm, rf_hbm,
    row_out, slab_out,
    sf, sv, rv, rf, rft, rsq, coup, slots, slabn, slabp, ssq, weights, wcol,
    kept, s_a, r_a, s_b, r_b,
    g_own, g_near, g_from, g_send, g_recv,
    in_sem, ag_send, ag_recv, g_ssem, g_rsem, near_sem, a_send, a_recv, b_send, b_recv,
):
    row, col = lax.axis_index("row"), lax.axis_index("col")
    z, lo = lax.rem(row, Z), row // Z
    y, hi, core = col // 4, lax.rem(col // 2, 2), lax.rem(col, 2)
    me = y * 2 + hi

    sibling = {"row": row, "col": col + 1 - 2 * core}
    neighbour = {"row": (1 - lo) * Z + z, "col": col}

    def z_peer(d):
        return lax.rem(z + d, Z)

    def along_z(d):
        return {"row": lo * Z + z_peer(d), "col": col}

    def column(d):
        index = lax.rem(y + d // 2, 4) * 2 + lax.rem(hi + d % 2, 2)
        return index, {"row": row, "col": index * 2 + core}

    loads = [
        pltpu.make_async_copy(src, dst, in_sem.at[i])
        for i, (src, dst) in enumerate(
            ((sf_hbm, sf), (sv_hbm, sv), (rv_hbm, rv), (rf_hbm, rf))
        )
    ]
    for load in loads:
        load.start()

    barrier = pltpu.get_barrier_semaphore()

    def greet(d, c):
        pl.semaphore_signal(barrier, inc=1, device_id=along_z(d))
        return c

    lax.fori_loop(1, Z, greet, 0)
    for other in [sibling, neighbour] + [column(d)[1] for d in range(1, 8)]:
        pl.semaphore_signal(barrier, inc=1, device_id=other)
    loads[0].wait()
    slots[row] = sf[...]
    pl.semaphore_wait(barrier, Z - 1 + 9)

    def gather(d):
        return pltpu.make_async_remote_copy(
            sf, slots.at[row], ag_send.at[d], ag_recv.at[row], device_id=along_z(d)
        )

    def piece(slot):
        return pltpu.make_async_remote_copy(
            slots.at[slot], slots.at[slot], ag_send.at[Z + lax.rem(slot, Z)],
            ag_recv.at[slot], device_id=neighbour,
        )

    def zigzag(k):
        return jnp.where(lax.rem(k, 2) == 1, (k + 1) // 2, Z - k // 2)

    def send_slab(k, c):
        gather(zigzag(Z - k)).start()
        return c

    lax.fori_loop(1, Z, send_slab, 0)
    piece(row).start()

    first = lax.broadcasted_iota(jnp.int32, (VECS, COLS), 0) == 0
    loads[1].wait()
    scaled = (sv[...].astype(F32) * jnp.where(first, 0.5, -0.5 / PROBES)).T.astype(BF16)
    loads[2].wait()
    loads[3].wait()

    def rows(q):
        return pl.ds(pl.multiple_of(q * RQ, RQ), RQ)

    def prepare(q, c):
        wide = rf[rows(q), :].astype(F32).T
        rsq[q] = jnp.sum(wide * wide, axis=0, keepdims=True) * (0.5 / D)
        rft[q] = wide.astype(BF16)
        coup[q] = jnp.dot(scaled, rv[:, rows(q)], preferred_element_type=F32)
        return c

    lax.fori_loop(0, CHUNKS, prepare, 0)
    wcol[...] = jnp.zeros_like(wcol)

    def hand_on(k, c):
        slot = lo * Z + z_peer(zigzag(k))
        pltpu.make_async_remote_copy(
            sf, slots.at[slot], ag_send.at[0], ag_recv.at[slot], device_id=neighbour
        ).wait_recv()
        piece(slot).start()
        return c

    lax.fori_loop(1, Z, hand_on, 0)

    def got_slab(d, c):
        piece((1 - lo) * Z + z_peer(d)).wait_recv()
        return c

    lax.fori_loop(0, Z, got_slab, 0)

    slab_t = slots[...].astype(F32).reshape(D, COLS)
    slab_n = slab_t.T
    ssq[...] = jnp.broadcast_to(
        jnp.sum(slab_n * slab_n, axis=1, keepdims=True) * (0.5 / D), ssq.shape
    )
    slabn[...] = (slab_n * (1.0 / D)).astype(BF16)
    order = [b * 2 + cc for cc in range(2) for b in range(8)]
    slabp[...] = jnp.concatenate(
        [slab_t[g * 16 : g * 16 + 16] * (1.0 / D) for g in order], axis=0
    ).astype(BF16)

    def hop_a(q):
        return pltpu.make_async_remote_copy(
            s_a.at[q], r_a.at[q], a_send.at[q], a_recv.at[q], device_id=sibling
        )

    def hop_b(q, d):
        index, to = column(d)
        return pltpu.make_async_remote_copy(
            s_b.at[q, index], r_b.at[q, me], b_send.at[q, d], b_recv.at[q, me],
            device_id=to,
        )

    def compute(q):
        feats = rft[q]
        inner = jnp.dot(slabn[...], feats, preferred_element_type=F32)
        gauss = jnp.exp(inner - rsq[q] - ssq[:, :1])
        w = (coup[q] * gauss).astype(BF16)
        wf = w.astype(F32)
        wide = jnp.sum(wf, axis=0, keepdims=True) * (1.0 / D)
        prod = jnp.dot(slabp[...], w, preferred_element_type=F32)
        halves = []
        for cc in range(2):
            own = jnp.concatenate(
                [
                    feats[g * 16 : g * 16 + 16].astype(F32)
                    for g in order[cc * 8 : cc * 8 + 8]
                ],
                axis=0,
            )
            halves.append(prod[cc * 128 : cc * 128 + 128] - wide * own)
        mine = core == 0
        s_a[q] = jnp.where(mine, halves[1], halves[0]).astype(BF16).reshape(8, 16, RQ)
        hop_a(q).start()
        kept[q] = jnp.where(mine, halves[0], halves[1]).reshape(8, 16, RQ)
        weights[q] = w
        part = wf[:, :128]
        for lane in range(128, RQ, 128):
            part = part + wf[:, lane : lane + 128]
        wcol[...] += part

    def stage_b(q):
        hop_a(q).wait_recv()
        total = kept[q] + r_a[q].astype(F32)
        s_b[q] = total.astype(BF16)
        for d in (5, 4, 3, 7, 1, 2, 6):
            hop_b(q, d).start()
        kept[q, me] = kept[q, me] + r_a[q, me].astype(F32)

    def step(t, c):
        compute(t)
        pl.when(t >= LAG)(lambda: stage_b(t - LAG))
        return c

    lax.fori_loop(0, CHUNKS, step, 0)

    near = pltpu.make_async_remote_copy(
        g_near, g_from, near_sem.at[0], near_sem.at[1], device_id=neighbour
    )

    def products(q, grad):
        return grad + jnp.dot(weights[q], rf[rows(q), :], preferred_element_type=F32)

    grad = lax.fori_loop(0, CHUNKS, products, jnp.zeros((COLS, D), F32))
    total = jnp.sum(wcol[...], axis=1, keepdims=True)
    grad = grad * (1.0 / D) - total * slabn[...].astype(F32)
    g_own[...] = grad.T.reshape(2, Z, 8, COLS)
    g_near[...] = g_own[1 - lo].astype(BF16)
    near.start()
    lax.fori_loop(CHUNKS - LAG, CHUNKS, lambda q, c: (stage_b(q), c)[1], 0)
    near.wait_recv()
    g_own[lo] = g_own[lo] + g_from[...].astype(F32)
    g_send[...] = g_own[lo].astype(BF16)

    def exchange(d):
        return pltpu.make_async_remote_copy(
            g_send.at[z_peer(d)], g_recv.at[z], g_ssem.at[d], g_rsem.at[z],
            device_id=along_z(d),
        )

    def send_grad(k, c):
        exchange(zigzag(Z - k)).start()
        return c

    lax.fori_loop(1, Z, send_grad, 0)
    g_recv[z] = jnp.zeros((8, COLS), BF16)

    def finish(q, c):
        total = kept[q, me]
        for d in (1, 2, 6, 3, 7, 4, 5):
            index = column(d)[0]
            pltpu.make_async_remote_copy(
                s_b.at[q, index], r_b.at[q, index], b_send.at[q, d],
                b_recv.at[q, index], device_id=sibling,
            ).wait_recv()
            total = total + r_b[q, index].astype(F32)
        row_out[:, rows(q)] = total
        return c

    lax.fori_loop(0, CHUNKS, finish, 0)

    def got_grad(d, c):
        peer = z_peer(d)
        pltpu.make_async_remote_copy(
            g_send.at[peer], g_recv.at[peer], g_ssem.at[d], g_rsem.at[peer],
            device_id=neighbour,
        ).wait_recv()
        return c

    lax.fori_loop(1, Z, got_grad, 0)
    slab_out[...] = g_own[lo, z] + jnp.sum(g_recv[...].astype(F32), axis=0)

    near.wait_send()

    def sent(d, c):
        gather(d).wait_send()
        exchange(d).wait_send()
        return c

    lax.fori_loop(1, Z, sent, 0)

    def sent_pieces(k, c):
        piece(lo * Z + k).wait_send()
        return c

    lax.fori_loop(0, Z, sent_pieces, 0)

    def sent_rows(q, c):
        hop_a(q).wait_send()
        for d in range(1, 8):
            hop_b(q, d).wait_send()
        return c

    lax.fori_loop(0, CHUNKS, sent_rows, 0)


def local(row_features, row_vectors, slab_features, slab_vectors):
    vmem = pl.BlockSpec(memory_space=pltpu.VMEM)
    hbm = pl.BlockSpec(memory_space=pltpu.MemorySpace.HBM)
    dma = pltpu.SemaphoreType.DMA
    part = lambda dtype: pltpu.VMEM((CHUNKS, 8, 16, RQ), dtype)
    row_t, slab_t = pl.pallas_call(
        kernel,
        out_shape=(
            jax.ShapeDtypeStruct((16, ROWS), F32),
            jax.ShapeDtypeStruct((8, COLS), F32),
        ),
        in_specs=[hbm, hbm, hbm, hbm],
        out_specs=(vmem, vmem),
        scratch_shapes=[
            pltpu.VMEM((8, COLS), BF16),
            pltpu.VMEM((VECS, COLS), BF16),
            pltpu.VMEM((VECS, ROWS), BF16),
            pltpu.VMEM((ROWS, D), BF16),
            pltpu.VMEM((CHUNKS, D, RQ), BF16),
            pltpu.VMEM((CHUNKS, 1, RQ), F32),
            pltpu.VMEM((CHUNKS, COLS, RQ), F32),
            pltpu.VMEM((N_ROW, 8, COLS), BF16),
            pltpu.VMEM((COLS, D), BF16),
            pltpu.VMEM((D, COLS), BF16),
            pltpu.VMEM((COLS, 128), F32),
            pltpu.VMEM((CHUNKS, COLS, RQ), BF16),
            pltpu.VMEM((COLS, 128), F32),
            part(F32), part(BF16), part(BF16), part(BF16), part(BF16),
            pltpu.VMEM((2, Z, 8, COLS), F32),
            pltpu.VMEM((Z, 8, COLS), BF16),
            pltpu.VMEM((Z, 8, COLS), BF16),
            pltpu.VMEM((Z, 8, COLS), BF16),
            pltpu.VMEM((Z, 8, COLS), BF16),
            dma((4,)), dma((2 * Z,)), dma((N_ROW,)), dma((Z,)), dma((Z,)), dma((2,)),
            dma((CHUNKS,)), dma((CHUNKS,)), dma((CHUNKS, 8)), dma((CHUNKS, 8)),
        ],
        compiler_params=pltpu.CompilerParams(
            collective_id=0, has_side_effects=True, vmem_limit_bytes=56 * 1024 * 1024
        ),
        cost_estimate=pl.CostEstimate(
            flops=3 * 2 * ROWS * COLS * D, bytes_accessed=4_000_000,
            transcendentals=ROWS * COLS,
        ),
    )(slab_features.T, slab_vectors, row_vectors, row_features)
    return row_t.T, slab_t.T


def solution(mesh):
    return jax.shard_map(
        local,
        mesh=mesh,
        in_specs=(P("row", None), P(None, "row"), P("col", "row"), P(None, "col")),
        out_specs=(P("row", "col"), P("col", "row")),
        check_vma=False,
    )
```

time: 311 us -> 46.7 us (0.15)
  waiting for transfers between devices: 219 us -> 0 us
  blocking collectives: 69.7 us -> 0 us
  Pallas kernels: 0 us -> 42.9 us
  between operations: 14.1 us -> 0.64 us
  matrix products: 5.17 us -> 0 us
    reduce_scatter x2 -> x0, waiting for transfers between devices: 219 us -> none  [the longest x1 124 us: local(): lax.psum_scatter(partial_slab, 'row', scatter_dimension=1, tiled=True)]
    all_gather x1 -> x0, blocking collectives: 69.7 us -> none  [local(): columns = lax.all_gather(slab_features, 'row', axis=1, tiled=True)]
    pallas_call x0 -> x1, Pallas kernels: none -> 42.9 us  [local(): pl.pallas_call(kernel, out_shape=(jax.ShapeDtypeStruct((16, ROWS), F32),...]
    dot_general x4 -> x0, matrix products: 5.17 us -> none  [the longest x1 2.27 us: local(): product = jnp.dot(weights, columns, preferred_element_type=jnp.float32)]
  transfers between devices with their start and end apart: 2 -> 0, of which waited for: 2 -> 0; matrix products, arithmetic and copies ran while one was open for 1% -> 0% of each run, Pallas kernels for 0% -> 0%
where the time goes in v2:
time: 46.7 us; the launch traced here: 46.4 us
  Pallas kernels  42.9 us (92%)
  local copies, waits for them, and re-layouts  2.91 us (6%)
  between operations  0.64 us (1%)
    pallas_call x1, Pallas kernels, local(): pl.pallas_call(kernel, out_shape=(jax.ShapeDtypeStruct((16, ROWS), F32),...  42.9 us
    unnamed x2, local copies, waits for them, and re-layouts  2.91 us

profile of v2, /device:TPU:8, one launch (start us, length us, event | category | flops | bytes accessed | tf_op | source)
XLA Modules:
  0.0 46.4 jit_solution(17541375020695061825)
XLA Ops:
  0.6 42.9 %shard_map.59 = (f32[16,3072]{1,0:T(8,128)}, f32[8,192]{1,0:T(8,128)}) custom-call(bf16[8,192]{1,0:T(8,128)(2,1)} %bitcast.5, bf16[17,192]{1,0:T(8,128)(2,1)} %sv_hbm.1, bf16[17,3072]{1,0:T(8,128)(2,1)} %rv_hbm.1, bf16[3072,256]{1,0:T(8,128)(2,1)} %rf_hbm.1), custom_call_target="tpu_custom_call" | custom-call | flops 905969664 | bytes 4000000 | tf_op jit(solution)/shard_map/pallas_call | solution.py:278
  43.5 1.6 %copy.8 = f32[3072,16]{0,1:T(8,128)} copy(f32[3072,16]{0,1:T(8,128)} %bitcast.3) | data formatting | bytes 393216
  45.1 1.3 %copy.9 = f32[192,8]{0,1:T(8,128)} copy(f32[192,8]{0,1:T(8,128)} %bitcast.4) | data formatting | bytes 12288

commit v3 on v2

--- a/solution.py
+++ b/solution.py
@@ -13,9 +13,9 @@
 ROWS = 3072
 COLS = 192
 N_ROW = 32
-CHUNKS = 3
+CHUNKS = 2
 RQ = ROWS // CHUNKS
-LAG = 3
+LAG = 2
 Z = 16
 F32, BF16 = jnp.float32, jnp.bfloat16
 
@@ -24,9 +24,9 @@
     sf_hbm, sv_hbm, rv_hbm, rf_hbm,
     row_out, slab_out,
     sf, sv, rv, rf, rft, rsq, coup, slots, slabn, slabp, ssq, weights, wcol,
-    kept, s_a, r_a, s_b, r_b,
+    kept, s_a, r_a, s_b, r_b, row_v, slab_v,
     g_own, g_near, g_from, g_send, g_recv,
-    in_sem, ag_send, ag_recv, g_ssem, g_rsem, near_sem, a_send, a_recv, b_send, b_recv,
+    in_sem, ag_send, ag_recv, g_ssem, g_rsem, near_sem, a_send, a_recv, b_send, b_recv, out_sem,
 ):
     row, col = lax.axis_index("row"), lax.axis_index("col")
     z, lo = lax.rem(row, Z), row // Z
@@ -221,6 +221,11 @@
     lax.fori_loop(1, Z, send_grad, 0)
     g_recv[z] = jnp.zeros((8, COLS), BF16)
 
+    def result(q):
+        return pltpu.make_async_copy(
+            row_v.at[:, rows(q)], row_out.at[:, rows(q)], out_sem.at[q]
+        )
+
     def finish(q, c):
         total = kept[q, me]
         for d in (1, 2, 6, 3, 7, 4, 5):
@@ -230,7 +235,8 @@
                 b_recv.at[q, index], device_id=sibling,
             ).wait_recv()
             total = total + r_b[q, index].astype(F32)
-        row_out[:, rows(q)] = total
+        row_v[:, rows(q)] = total
+        result(q).start()
         return c
 
     lax.fori_loop(0, CHUNKS, finish, 0)
@@ -244,7 +250,12 @@
         return c
 
     lax.fori_loop(1, Z, got_grad, 0)
-    slab_out[...] = g_own[lo, z] + jnp.sum(g_recv[...].astype(F32), axis=0)
+    slab_v[...] = g_own[lo, z] + jnp.sum(g_recv[...].astype(F32), axis=0)
+    slab_result = pltpu.make_async_copy(slab_v, slab_out, out_sem.at[CHUNKS])
+    slab_result.start()
+    for q in range(CHUNKS):
+        result(q).wait()
+    slab_result.wait()
 
     near.wait_send()
 
@@ -268,6 +279,11 @@
         return c
 
     lax.fori_loop(0, CHUNKS, sent_rows, 0)
+
+
+def place(row_in, slab_in, row_out, slab_out):
+    row_out[...] = row_in[...]
+    slab_out[...] = slab_in[...]
 
 
 def local(row_features, row_vectors, slab_features, slab_vectors):
@@ -282,7 +298,7 @@
             jax.ShapeDtypeStruct((8, COLS), F32),
         ),
         in_specs=[hbm, hbm, hbm, hbm],
-        out_specs=(vmem, vmem),
+        out_specs=(hbm, hbm),
         scratch_shapes=[
             pltpu.VMEM((8, COLS), BF16),
             pltpu.VMEM((VECS, COLS), BF16),
@@ -298,13 +314,14 @@
             pltpu.VMEM((CHUNKS, COLS, RQ), BF16),
             pltpu.VMEM((COLS, 128), F32),
             part(F32), part(BF16), part(BF16), part(BF16), part(BF16),
+            pltpu.VMEM((16, ROWS), F32), pltpu.VMEM((8, COLS), F32),
             pltpu.VMEM((2, Z, 8, COLS), F32),
             pltpu.VMEM((Z, 8, COLS), BF16),
             pltpu.VMEM((Z, 8, COLS), BF16),
             pltpu.VMEM((Z, 8, COLS), BF16),
             pltpu.VMEM((Z, 8, COLS), BF16),
             dma((4,)), dma((2 * Z,)), dma((N_ROW,)), dma((Z,)), dma((Z,)), dma((2,)),
-            dma((CHUNKS,)), dma((CHUNKS,)), dma((CHUNKS, 8)), dma((CHUNKS, 8)),
+            dma((CHUNKS,)), dma((CHUNKS,)), dma((CHUNKS, 8)), dma((CHUNKS, 8)), dma((CHUNKS + 1,)),
         ],
         compiler_params=pltpu.CompilerParams(
             collective_id=0, has_side_effects=True, vmem_limit_bytes=56 * 1024 * 1024
@@ -314,6 +331,16 @@
             transcendentals=ROWS * COLS,
         ),
     )(slab_features.T, slab_vectors, row_vectors, row_features)
+    row_t, slab_t = pl.pallas_call(
+        place,
+        out_shape=(
+            jax.ShapeDtypeStruct((16, ROWS), F32),
+            jax.ShapeDtypeStruct((8, COLS), F32),
+        ),
+        in_specs=[vmem, vmem],
+        out_specs=(vmem, vmem),
+        compiler_params=pltpu.CompilerParams(vmem_limit_bytes=56 * 1024 * 1024),
+    )(row_t, slab_t)
     return row_t.T, slab_t.T
 
 

time: 46.7 us -> 45.1 us (0.966)
  local copies, waits for them, and re-layouts: 2.91 us -> 0 us
  Pallas kernels: 42.9 us -> 44.3 us
    unnamed x2 -> x0, local copies, waits for them, and re-layouts: 2.91 us -> none
    pallas_call x0 -> x1, Pallas kernels: none -> 1.62 us  [local(): pl.pallas_call(place, out_shape=(jax.ShapeDtypeStruct((16, ROWS), F32), j...]
where the time goes in v3:
time: 45.1 us; the launch traced here: 45 us
  Pallas kernels  44.3 us (98%)
  between operations  0.64 us (1%)
    pallas_call x1, Pallas kernels, local(): pl.pallas_call(kernel, out_shape=(jax.ShapeDtypeStruct((16, ROWS), F32),...  42.7 us
    pallas_call x1, Pallas kernels, local(): pl.pallas_call(place, out_shape=(jax.ShapeDtypeStruct((16, ROWS), F32), j...  1.62 us

profile of v3, /device:TPU:8, one launch (start us, length us, event | category | flops | bytes accessed | tf_op | source)
XLA Modules:
  0.0 45.0 jit_solution(17785166590694864547)
XLA Ops:
  0.6 42.7 %shard_map.59 = (f32[16,3072]{1,0:T(8,128)}, f32[8,192]{1,0:T(8,128)}) custom-call(bf16[8,192]{1,0:T(8,128)(2,1)} %bitcast.5, bf16[17,192]{1,0:T(8,128)(2,1)} %sv_hbm.1, bf16[17,3072]{1,0:T(8,128)(2,1)} %rv_hbm.1, bf16[3072,256]{1,0:T(8,128)(2,1)} %rf_hbm.1), custom_call_target="tpu_custom_call" | custom-call | flops 905969664 | bytes 4000000 | tf_op jit(solution)/shard_map/pallas_call | solution.py:294
  43.4 1.6 %shard_map.60 = (f32[16,3072]{1,0:T(8,128)}, f32[8,192]{1,0:T(8,128)}) custom-call(f32[16,3072]{1,0:T(8,128)} %get-tuple-element.6.row_in, f32[8,192]{1,0:T(8,128)} %get-tuple-element.7.slab_in), custom_call_target="tpu_custom_call" | custom-call | tf_op jit(solution)/shard_map/pallas_call | solution.py:334

commit v4 on v3

--- a/solution.py
+++ b/solution.py
@@ -16,6 +16,7 @@
 CHUNKS = 2
 RQ = ROWS // CHUNKS
 LAG = 2
+NEAR = 7
 Z = 16
 F32, BF16 = jnp.float32, jnp.bfloat16
 
@@ -42,6 +43,9 @@
     def along_z(d):
         return {"row": lo * Z + z_peer(d), "col": col}
 
+    def beside_z(d):
+        return {"row": (1 - lo) * Z + z_peer(d), "col": col}
+
     def column(d):
         index = lax.rem(y + d // 2, 4) * 2 + lax.rem(hi + d % 2, 2)
         return index, {"row": row, "col": index * 2 + core}
@@ -57,16 +61,25 @@
 
     barrier = pltpu.get_barrier_semaphore()
 
-    def greet(d, c):
-        pl.semaphore_signal(barrier, inc=1, device_id=along_z(d))
-        return c
-
+    def zigzag(k):
+        return jnp.where(lax.rem(k, 2) == 1, (k + 1) // 2, Z - k // 2)
+
+    def greet(k, c):
+        pl.semaphore_signal(barrier, inc=1, device_id=along_z(zigzag(Z - k)))
+        return c
+
+    def greet_far(k, c):
+        pl.semaphore_signal(barrier, inc=1, device_id=beside_z(zigzag(Z - k)))
+        return c
+
+    FAR = Z - 1 - 2 * NEAR
+    lax.fori_loop(1, FAR + 1, greet_far, 0)
     lax.fori_loop(1, Z, greet, 0)
-    for other in [sibling, neighbour] + [column(d)[1] for d in range(1, 8)]:
+    for other in [column(d)[1] for d in (5, 4, 3, 7, 1, 2, 6)] + [neighbour, sibling]:
         pl.semaphore_signal(barrier, inc=1, device_id=other)
     loads[0].wait()
     slots[row] = sf[...]
-    pl.semaphore_wait(barrier, Z - 1 + 9)
+    pl.semaphore_wait(barrier, Z - 1 + FAR + 9)
 
     def gather(d):
         return pltpu.make_async_remote_copy(
@@ -79,14 +92,23 @@
             ag_recv.at[slot], device_id=neighbour,
         )
 
-    def zigzag(k):
-        return jnp.where(lax.rem(k, 2) == 1, (k + 1) // 2, Z - k // 2)
-
-    def send_slab(k, c):
+    def gather_far(d):
+        return pltpu.make_async_remote_copy(
+            sf, slots.at[row], ag_send.at[2 * Z + d], ag_recv.at[row],
+            device_id=beside_z(d),
+        )
+
+    def send_far(k, c):
+        gather_far(zigzag(Z - k)).start()
         gather(zigzag(Z - k)).start()
         return c
 
-    lax.fori_loop(1, Z, send_slab, 0)
+    def send_near(k, c):
+        gather(zigzag(Z - k)).start()
+        return c
+
+    lax.fori_loop(1, FAR + 1, send_far, 0)
+    lax.fori_loop(FAR + 1, Z, send_near, 0)
     piece(row).start()
 
     first = lax.broadcasted_iota(jnp.int32, (VECS, COLS), 0) == 0
@@ -116,13 +138,23 @@
         piece(slot).start()
         return c
 
-    lax.fori_loop(1, Z, hand_on, 0)
-
-    def got_slab(d, c):
-        piece((1 - lo) * Z + z_peer(d)).wait_recv()
-        return c
-
-    lax.fori_loop(0, Z, got_slab, 0)
+    lax.fori_loop(1, 2 * NEAR + 1, hand_on, 0)
+
+    def arrived(slot):
+        pltpu.make_async_remote_copy(
+            sf, slots.at[slot], ag_send.at[0], ag_recv.at[slot], device_id=neighbour
+        ).wait_recv()
+
+    def got_far(k, c):
+        arrived(lo * Z + z_peer(zigzag(k)))
+        return c
+
+    def got_beside(d, c):
+        arrived((1 - lo) * Z + z_peer(d))
+        return c
+
+    lax.fori_loop(2 * NEAR + 1, Z, got_far, 0)
+    lax.fori_loop(0, Z, got_beside, 0)
 
     slab_t = slots[...].astype(F32).reshape(D, COLS)
     slab_n = slab_t.T
@@ -130,10 +162,21 @@
         jnp.sum(slab_n * slab_n, axis=1, keepdims=True) * (0.5 / D), ssq.shape
     )
     slabn[...] = (slab_n * (1.0 / D)).astype(BF16)
-    order = [b * 2 + cc for cc in range(2) for b in range(8)]
-    slabp[...] = jnp.concatenate(
-        [slab_t[g * 16 : g * 16 + 16] * (1.0 / D) for g in order], axis=0
-    ).astype(BF16)
+    for half in range(2):
+        at = pl.multiple_of(lax.rem(half + core, 2) * (D // 2), D // 2)
+        slabp[pl.ds(at, D // 2)] = jnp.concatenate(
+            [slab_t[b * 32 + half * 16 : b * 32 + half * 16 + 16] * (1.0 / D) for b in range(8)],
+            axis=0,
+        ).astype(BF16)
+
+    def half_of(q, which):
+        return jnp.concatenate(
+            [
+                rft[q, pl.ds(pl.multiple_of(b * 32 + which * 16, 16), 16)].astype(F32)
+                for b in range(8)
+            ],
+            axis=0,
+        )
 
     def hop_a(q):
         return pltpu.make_async_remote_copy(
@@ -155,20 +198,10 @@
         wf = w.astype(F32)
         wide = jnp.sum(wf, axis=0, keepdims=True) * (1.0 / D)
         prod = jnp.dot(slabp[...], w, preferred_element_type=F32)
-        halves = []
-        for cc in range(2):
-            own = jnp.concatenate(
-                [
-                    feats[g * 16 : g * 16 + 16].astype(F32)
-                    for g in order[cc * 8 : cc * 8 + 8]
-                ],
-                axis=0,
-            )
-            halves.append(prod[cc * 128 : cc * 128 + 128] - wide * own)
-        mine = core == 0
-        s_a[q] = jnp.where(mine, halves[1], halves[0]).astype(BF16).reshape(8, 16, RQ)
+        theirs = prod[D // 2 :] - wide * half_of(q, 1 - core)
+        s_a[q] = theirs.astype(BF16).reshape(8, 16, RQ)
         hop_a(q).start()
-        kept[q] = jnp.where(mine, halves[0], halves[1]).reshape(8, 16, RQ)
+        kept[q] = (prod[: D // 2] - wide * half_of(q, core)).reshape(8, 16, RQ)
         weights[q] = w
         part = wf[:, :128]
         for lane in range(128, RQ, 128):
@@ -203,7 +236,7 @@
     g_own[...] = grad.T.reshape(2, Z, 8, COLS)
     g_near[...] = g_own[1 - lo].astype(BF16)
     near.start()
-    lax.fori_loop(CHUNKS - LAG, CHUNKS, lambda q, c: (stage_b(q), c)[1], 0)
+    lax.fori_loop(0, 1, lambda q, c: (stage_b(q), c)[1], 0)
     near.wait_recv()
     g_own[lo] = g_own[lo] + g_from[...].astype(F32)
     g_send[...] = g_own[lo].astype(BF16)
@@ -219,7 +252,39 @@
         return c
 
     lax.fori_loop(1, Z, send_grad, 0)
+    lax.fori_loop(1, CHUNKS, lambda q, c: (stage_b(q), c)[1], 0)
     g_recv[z] = jnp.zeros((8, COLS), BF16)
+
+    near.wait_send()
+
+    def sent(d, c):
+        gather(d).wait_send()
+        return c
+
+    lax.fori_loop(1, Z, sent, 0)
+
+    def sent_far(k, c):
+        gather_far(zigzag(Z - k)).wait_send()
+        return c
+
+    lax.fori_loop(1, FAR + 1, sent_far, 0)
+
+    def sent_pieces(k, c):
+        piece(lo * Z + z_peer(zigzag(k))).wait_send()
+        return c
+
+    lax.fori_loop(1, 2 * NEAR + 1, sent_pieces, 0)
+    piece(row).wait_send()
+
+    def sent_rows(q, c):
+        hop_a(q).wait_send()
+        for d in range(1, 8):
+            hop_b(q, d).wait_send()
+        return c
+
+    def sent_grad(d, c):
+        exchange(d).wait_send()
+        return c
 
     def result(q):
         return pltpu.make_async_copy(
@@ -239,7 +304,10 @@
         result(q).start()
         return c
 
-    lax.fori_loop(0, CHUNKS, finish, 0)
+    lax.fori_loop(0, CHUNKS - 1, finish, 0)
+    lax.fori_loop(0, CHUNKS, sent_rows, 0)
+    lax.fori_loop(1, Z, sent_grad, 0)
+    finish(CHUNKS - 1, 0)
 
     def got_grad(d, c):
         peer = z_peer(d)
@@ -256,29 +324,6 @@
     for q in range(CHUNKS):
         result(q).wait()
     slab_result.wait()
-
-    near.wait_send()
-
-    def sent(d, c):
-        gather(d).wait_send()
-        exchange(d).wait_send()
-        return c
-
-    lax.fori_loop(1, Z, sent, 0)
-
-    def sent_pieces(k, c):
-        piece(lo * Z + k).wait_send()
-        return c
-
-    lax.fori_loop(0, Z, sent_pieces, 0)
-
-    def sent_rows(q, c):
-        hop_a(q).wait_send()
-        for d in range(1, 8):
-            hop_b(q, d).wait_send()
-        return c
-
-    lax.fori_loop(0, CHUNKS, sent_rows, 0)
 
 
 def place(row_in, slab_in, row_out, slab_out):
@@ -320,7 +365,7 @@
             pltpu.VMEM((Z, 8, COLS), BF16),
             pltpu.VMEM((Z, 8, COLS), BF16),
             pltpu.VMEM((Z, 8, COLS), BF16),
-            dma((4,)), dma((2 * Z,)), dma((N_ROW,)), dma((Z,)), dma((Z,)), dma((2,)),
+            dma((4,)), dma((3 * Z,)), dma((N_ROW,)), dma((Z,)), dma((Z,)), dma((2,)),
             dma((CHUNKS,)), dma((CHUNKS,)), dma((CHUNKS, 8)), dma((CHUNKS, 8)), dma((CHUNKS + 1,)),
         ],
         compiler_params=pltpu.CompilerParams(

time: 45.1 us -> 45.1 us (level)
  no operation moved by 1% of the time
where the time goes in v4:
time: 45.1 us; the launch traced here: 45 us
  Pallas kernels  44.3 us (98%)
  between operations  0.64 us (1%)
    pallas_call x1, Pallas kernels, local(): pl.pallas_call(kernel, out_shape=(jax.ShapeDtypeStruct((16, ROWS), F32),...  42.7 us
    pallas_call x1, Pallas kernels, local(): pl.pallas_call(place, out_shape=(jax.ShapeDtypeStruct((16, ROWS), F32), j...  1.62 us

profile of v4, /device:TPU:8, one launch (start us, length us, event | category | flops | bytes accessed | tf_op | source)
XLA Modules:
  0.0 45.0 jit_solution(1983118037212439666)
XLA Ops:
  0.6 42.7 %shard_map.59 = (f32[16,3072]{1,0:T(8,128)}, f32[8,192]{1,0:T(8,128)}) custom-call(bf16[8,192]{1,0:T(8,128)(2,1)} %bitcast.5, bf16[17,192]{1,0:T(8,128)(2,1)} %sv_hbm.1, bf16[17,3072]{1,0:T(8,128)(2,1)} %rv_hbm.1, bf16[3072,256]{1,0:T(8,128)(2,1)} %rf_hbm.1), custom_call_target="tpu_custom_call" | custom-call | flops 905969664 | bytes 4000000 | tf_op jit(solution)/shard_map/pallas_call | solution.py:339
  43.4 1.6 %shard_map.60 = (f32[16,3072]{1,0:T(8,128)}, f32[8,192]{1,0:T(8,128)}) custom-call(f32[16,3072]{1,0:T(8,128)} %get-tuple-element.6.row_in, f32[8,192]{1,0:T(8,128)} %get-tuple-element.7.slab_in), custom_call_target="tpu_custom_call" | custom-call | tf_op jit(solution)/shard_map/pallas_call | solution.py:379

commit v5 on v3

--- a/solution.py
+++ b/solution.py
@@ -130,10 +130,21 @@
         jnp.sum(slab_n * slab_n, axis=1, keepdims=True) * (0.5 / D), ssq.shape
     )
     slabn[...] = (slab_n * (1.0 / D)).astype(BF16)
-    order = [b * 2 + cc for cc in range(2) for b in range(8)]
-    slabp[...] = jnp.concatenate(
-        [slab_t[g * 16 : g * 16 + 16] * (1.0 / D) for g in order], axis=0
-    ).astype(BF16)
+    for half in range(2):
+        at = pl.multiple_of(lax.rem(half + core, 2) * (D // 2), D // 2)
+        slabp[pl.ds(at, D // 2)] = jnp.concatenate(
+            [slab_t[b * 32 + half * 16 : b * 32 + half * 16 + 16] * (1.0 / D) for b in range(8)],
+            axis=0,
+        ).astype(BF16)
+
+    def half_of(q, which):
+        return jnp.concatenate(
+            [
+                rft[q, pl.ds(pl.multiple_of(b * 32 + which * 16, 16), 16)].astype(F32)
+                for b in range(8)
+            ],
+            axis=0,
+        )
 
     def hop_a(q):
         return pltpu.make_async_remote_copy(
@@ -155,20 +166,10 @@
         wf = w.astype(F32)
         wide = jnp.sum(wf, axis=0, keepdims=True) * (1.0 / D)
         prod = jnp.dot(slabp[...], w, preferred_element_type=F32)
-        halves = []
-        for cc in range(2):
-            own = jnp.concatenate(
-                [
-                    feats[g * 16 : g * 16 + 16].astype(F32)
-                    for g in order[cc * 8 : cc * 8 + 8]
-                ],
-                axis=0,
-            )
-            halves.append(prod[cc * 128 : cc * 128 + 128] - wide * own)
-        mine = core == 0
-        s_a[q] = jnp.where(mine, halves[1], halves[0]).astype(BF16).reshape(8, 16, RQ)
+        theirs = prod[D // 2 :] - wide * half_of(q, 1 - core)
+        s_a[q] = theirs.astype(BF16).reshape(8, 16, RQ)
         hop_a(q).start()
-        kept[q] = jnp.where(mine, halves[0], halves[1]).reshape(8, 16, RQ)
+        kept[q] = (prod[: D // 2] - wide * half_of(q, core)).reshape(8, 16, RQ)
         weights[q] = w
         part = wf[:, :128]
         for lane in range(128, RQ, 128):

time: 45.1 us -> 45.1 us (level)
  no operation moved by 1% of the time
where the time goes in v5:
time: 45.1 us; the launch traced here: 45 us
  Pallas kernels  44.4 us (98%)
  between operations  0.64 us (1%)
    pallas_call x1, Pallas kernels, local(): pl.pallas_call(kernel, out_shape=(jax.ShapeDtypeStruct((16, ROWS), F32),...  42.7 us
    pallas_call x1, Pallas kernels, local(): pl.pallas_call(place, out_shape=(jax.ShapeDtypeStruct((16, ROWS), F32), j...  1.62 us

profile of v5, /device:TPU:8, one launch (start us, length us, event | category | flops | bytes accessed | tf_op | source)
XLA Modules:
  0.0 45.0 jit_solution(16490300548026940267)
XLA Ops:
  0.6 42.7 %shard_map.59 = (f32[16,3072]{1,0:T(8,128)}, f32[8,192]{1,0:T(8,128)}) custom-call(bf16[8,192]{1,0:T(8,128)(2,1)} %bitcast.5, bf16[17,192]{1,0:T(8,128)(2,1)} %sv_hbm.1, bf16[17,3072]{1,0:T(8,128)(2,1)} %rv_hbm.1, bf16[3072,256]{1,0:T(8,128)(2,1)} %rf_hbm.1), custom_call_target="tpu_custom_call" | custom-call | flops 905969664 | bytes 4000000 | tf_op jit(solution)/shard_map/pallas_call | solution.py:295
  43.4 1.6 %shard_map.60 = (f32[16,3072]{1,0:T(8,128)}, f32[8,192]{1,0:T(8,128)}) custom-call(f32[16,3072]{1,0:T(8,128)} %get-tuple-element.6.row_in, f32[8,192]{1,0:T(8,128)} %get-tuple-element.7.slab_in), custom_call_target="tpu_custom_call" | custom-call | tf_op jit(solution)/shard_map/pallas_call | solution.py:335

commit v6 on v5

--- a/solution.py
+++ b/solution.py
@@ -57,8 +57,11 @@
 
     barrier = pltpu.get_barrier_semaphore()
 
-    def greet(d, c):
-        pl.semaphore_signal(barrier, inc=1, device_id=along_z(d))
+    def zigzag(k):
+        return jnp.where(lax.rem(k, 2) == 1, (k + 1) // 2, Z - k // 2)
+
+    def greet(k, c):
+        pl.semaphore_signal(barrier, inc=1, device_id=along_z(zigzag(Z - k)))
         return c
 
     lax.fori_loop(1, Z, greet, 0)
@@ -78,9 +81,6 @@
             slots.at[slot], slots.at[slot], ag_send.at[Z + lax.rem(slot, Z)],
             ag_recv.at[slot], device_id=neighbour,
         )
-
-    def zigzag(k):
-        return jnp.where(lax.rem(k, 2) == 1, (k + 1) // 2, Z - k // 2)
 
     def send_slab(k, c):
         gather(zigzag(Z - k)).start()

time: 45.1 us -> 45.1 us (level)
  no operation moved by 1% of the time
where the time goes in v6:
time: 45.1 us; the launch traced here: 44.9 us
  Pallas kernels  44.3 us (98%)
  between operations  0.64 us (1%)
    pallas_call x1, Pallas kernels, local(): pl.pallas_call(kernel, out_shape=(jax.ShapeDtypeStruct((16, ROWS), F32),...  42.7 us
    pallas_call x1, Pallas kernels, local(): pl.pallas_call(place, out_shape=(jax.ShapeDtypeStruct((16, ROWS), F32), j...  1.62 us

profile of v6, /device:TPU:8, one launch (start us, length us, event | category | flops | bytes accessed | tf_op | source)
XLA Modules:
  0.0 44.9 jit_solution(2597407946327036613)
XLA Ops:
  0.6 42.7 %shard_map.59 = (f32[16,3072]{1,0:T(8,128)}, f32[8,192]{1,0:T(8,128)}) custom-call(bf16[8,192]{1,0:T(8,128)(2,1)} %bitcast.5, bf16[17,192]{1,0:T(8,128)(2,1)} %sv_hbm.1, bf16[17,3072]{1,0:T(8,128)(2,1)} %rv_hbm.1, bf16[3072,256]{1,0:T(8,128)(2,1)} %rf_hbm.1), custom_call_target="tpu_custom_call" | custom-call | flops 905969664 | bytes 4000000 | tf_op jit(solution)/shard_map/pallas_call | solution.py:295
  43.3 1.6 %shard_map.60 = (f32[16,3072]{1,0:T(8,128)}, f32[8,192]{1,0:T(8,128)}) custom-call(f32[16,3072]{1,0:T(8,128)} %get-tuple-element.6.row_in, f32[8,192]{1,0:T(8,128)} %get-tuple-element.7.slab_in), custom_call_target="tpu_custom_call" | custom-call | tf_op jit(solution)/shard_map/pallas_call | solution.py:335
